TPU v7x, 512 devices: a whole 4x4x16 slice. The times are simulated.
512 devices in a mesh: seq: 32 (over z, core), head: 16 (over y, x).
Axes of the slice: x: 4, y: 4, z: 16, core: 2. Of those that a mesh axis runs over, the one named last changes fastest.
Arguments:
- inputs: float32 [131072, 2048], P('seq', 'head'), may hold values from -0.8 to 0.8
- b_proj: float32 [131072, 256], P('seq', 'head'), may hold values from -0.5 to 0.5
- c_proj: float32 [131072, 256], P('seq', 'head'), may hold values from -0.5 to 0.5
- log_decay: float32 [131072, 32], P('seq', 'head'), may hold values from -2 to 0, as said below
Outputs:
- outputs: float32 [131072, 2048], P('seq', 'head')
Inputs may be any that keep to these rules, and one draw needn't show every extreme that they name: log_decay is negative.
All inputs are finite; a program needn't handle non-finite values.
Results may differ from a plain program's by a relative error of at most 0.00011.
Values sent between devices are 32-bit elements; how exact they have to be, the bound alone decides.
A program may use at most 128 MiB of HBM per device.

v0:
```python
import jax
import jax.numpy as jnp
from jax import lax
from jax.sharding import PartitionSpec as P

BLOCK_LEN = 256


def prefix(part, axis, combine, identity, reverse):
    count = lax.axis_size(axis)
    place = lax.axis_index(axis)
    ahead = count - 1 - place if reverse else place
    gathered = jax.tree.map(lambda a: lax.all_gather(a, axis), part)
    state = jax.tree.map(lambda a, e: jnp.zeros_like(a) + jnp.asarray(e, a.dtype), part, identity)

    def one(step, state):
        source = count - 1 - step if reverse else step
        return combine(
            state, jax.tree.map(lambda a: lax.dynamic_index_in_dim(a, source, 0, False), gathered)
        )

    return lax.fori_loop(0, ahead, one, state)


def from_root(value, axis, source):
    kept = jnp.where(lax.axis_index(axis) == source, value, 0).astype(value.dtype)
    return lax.psum(kept, axis)


def combine(earlier, later):
    return (earlier[0] + later[0], jnp.exp(later[0])[:, None, None] * earlier[1] + later[1])


def upper_chain(pair, zero_pair):
    return prefix(pair, "seq", combine, zero_pair, True)


def on_device(inputs, b_proj, c_proj, log_decay):
    highest_value = lax.Precision.HIGHEST
    tokens_here = inputs.shape[0]
    heads_here = log_decay.shape[1]
    head_width = inputs.shape[1] // heads_here
    b_full, c_full = (
        lax.all_gather(b_proj, "head", axis=1, tiled=True),
        lax.all_gather(c_proj, "head", axis=1, tiled=True),
    )
    state_width = b_full.shape[1]
    blocks_here = tokens_here // BLOCK_LEN
    per_half = blocks_here // 2
    values = inputs.reshape(blocks_here, BLOCK_LEN, heads_here, head_width)
    b_blocks = b_full.reshape(blocks_here, BLOCK_LEN, state_width)
    c_blocks = c_full.reshape(blocks_here, BLOCK_LEN, state_width)
    decays = log_decay.reshape(blocks_here, BLOCK_LEN, heads_here)
    rows = lax.broadcasted_iota(jnp.int32, (BLOCK_LEN, BLOCK_LEN), 0)
    cols = lax.broadcasted_iota(jnp.int32, (BLOCK_LEN, BLOCK_LEN), 1)
    lower_mask = rows >= cols
    cumulative = jnp.einsum(
        "ts,gsh->gth", lower_mask.astype(jnp.float32), decays, precision=highest_value
    )
    ending = cumulative[:, -1, :]
    to_end = jnp.exp(ending[:, None, :] - cumulative)
    block_states = jnp.einsum(
        "gshp,gsn->ghpn", values * to_end[..., None], b_blocks, precision=highest_value
    )
    scores = jnp.einsum("gtn,gsn->gts", c_blocks, b_blocks, precision=highest_value)
    kernel_breadth = cumulative[:, :, None, :] - cumulative[:, None, :, :]
    weights = (
        jnp.exp(jnp.where(lower_mask[None, :, :, None], kernel_breadth, -jnp.inf))
        * scores[..., None]
    )
    inside = jnp.einsum("gtsh,gshp->gthp", weights, values, precision=highest_value)
    zero_pair = (
        jnp.zeros((heads_here,), jnp.float32),
        jnp.zeros((heads_here, head_width, state_width), jnp.float32),
    )
    prefix_logs = []
    prefix_states = []
    summaries = []
    for half_index in range(2):
        running = zero_pair
        for step_index in range(per_half):
            block_index = half_index * per_half + step_index
            prefix_logs.append(running[0])
            prefix_states.append(running[1])
            running = combine(running, (ending[block_index], block_states[block_index]))
        summaries.append(running)
    local_logs = jnp.stack(prefix_logs)
    local_states = jnp.stack(prefix_states)
    lower_pair = summaries[0]
    upper_pair = summaries[1]
    last_device = lax.axis_size("seq") - 1
    incoming_lower = prefix(lower_pair, "seq", combine, zero_pair, False)
    inclusive_pair = combine(incoming_lower, lower_pair)
    total_pair = (
        from_root(inclusive_pair[0], "seq", last_device),
        from_root(inclusive_pair[1], "seq", last_device),
    )
    incoming_upper = upper_chain(upper_pair, zero_pair)
    start_upper = combine(total_pair, incoming_upper)
    half_states = jnp.stack([incoming_lower[1], start_upper[1]])
    repeated = jnp.repeat(half_states, per_half, axis=0)
    entering = jnp.exp(local_logs)[:, :, None, None] * repeated + local_states
    carried = jnp.exp(cumulative)[..., None] * jnp.einsum(
        "ghpn,gtn->gthp", entering, c_blocks, precision=highest_value
    )
    return (inside + carried).reshape(tokens_here, heads_here * head_width)


def solution(mesh):
    return jax.shard_map(
        on_device,
        mesh=mesh,
        in_specs=(P("seq", "head"), P("seq", "head"), P("seq", "head"), P("seq", "head")),
        out_specs=P("seq", "head"),
        check_vma=False,
    )
```

profile of v0, /device:TPU:1, one launch (start us, length us, event | category | flops | bytes accessed | tf_op | source)
XLA Modules:
  0.0 521.8 jit_solution(14481283132890314328)
XLA Ops:
  8.1 1.9 copy.35
  12.5 1.6 broadcast_multiply_fusion
  14.1 68.4 %all-gather.9.cloned.1.call-done = f32[4096,256]{0,1:T(8,128)} async-done(((f32[4096,16]{0,1:T(8,128)}), f32[4096,256]{0,1:T(8,128)}) %all-gather.9.cloned.1.call-update) | async-done | bytes 4194320 | tf_op jit(solution)/shard_map/all_gather | solution.py:44
  82.5 5.6 %copy.34 = f32[4096,256]{1,0:T(8,128)} copy(f32[4096,256]{0,1:T(8,128)} %all-gather.9.cloned.1.call-done) | data formatting | bytes 8388608 | tf_op jit(solution)/shard_map/all_gather | solution.py:44
  88.2 6.4 %fusion.12 = f32[16,2,64,256]{3,2,1,0:T(8,128)S(1)} fusion(f32[16,256,256,1]{2,1,3,0:T(8,128)} %bitcast.169, f32[16,256,2,64]{1,0,3,2:T(8,128)} %broadcast_multiply_fusion), kind=kOutput, calls=%fused_computation.20 | convolution fusion | flops 1610612736 | bytes 8388608 | tf_op jit(solution)/shard_map/gshp,gsn->ghpn/dot_general | solution.py:62
  102.6 31.3 %all-gather.1 = f32[32,1,2]{2,1,0:T(1,128)S(1)} all-gather(f32[1,1,2]{2,1,0:T(1,128)S(1)} %get-tuple-element.236), channel_id=1, replica_groups=mesh['seq'=32,'head'=16] {'seq'}, dimensions={0}, use_global_device_ids=true | all-gather | bytes 264 | tf_op jit(solution)/shard_map/all_gather | solution.py:13
  133.9 28.1 %all-gather = f32[32,1,2]{2,1,0:T(1,128)S(1)} all-gather(f32[1,1,2]{2,1,0:T(1,128)S(1)} %get-tuple-element.225), channel_id=1, replica_groups=mesh['seq'=32,'head'=16] {'seq'}, dimensions={0}, use_global_device_ids=true | all-gather | bytes 264 | tf_op jit(solution)/shard_map/all_gather | solution.py:13
  162.1 5.6 %copy.33 = f32[4096,256]{1,0:T(8,128)} copy(f32[4096,256]{0,1:T(8,128)} %all-gather.7.cloned.1.call-done) | data formatting | bytes 8388608 | tf_op jit(solution)/shard_map/all_gather | solution.py:45
  171.9 11.6 %fusion.33 = f32[16,256,256]{2,1,0:T(8,128)S(1)} fusion(f32[16,256,256]{2,1,0:T(8,128)} %bitcast.167, f32[16,256,256]{2,1,0:T(8,128)} %bitcast.170), kind=kOutput, calls=%fused_computation.133 | convolution fusion | flops 3221225472 | bytes 12582912 | tf_op jit(solution)/shard_map/gtn,gsn->gts/dot_general | solution.py:65
  183.5 11.8 %fusion = f32[16,2,256,64]{2,3,1,0:T(8,128)} fusion(f32[16,256,256]{2,1,0:T(8,128)S(1)} %fusion.33, f32[16,256,2]{1,2,0:T(2,128)S(1)} %copy.31, pred[256,256]{1,0:T(8,128)(4,1)S(1)} %iota_compare_fusion, f32[16,256,2,64]{1,0,3,2:T(8,128)S(1)} %bitcast.173), kind=kOutput, calls=%fused_computation.6 | convolution fusion | flops 1616904192 | bytes 8486912 | tf_op jit(solution)/shard_map/gtsh,gshp->gthp/dot_general | solution.py:71
  195.2 33.2 %all-gather.11.cloned.1.call-done = f32[32,2,64,256]{3,2,1,0:T(8,128)} async-done(((f32[1,2,64,256]{3,2,1,0:T(8,128)}), f32[32,2,64,256]{3,2,1,0:T(8,128)}) %all-gather.11.cloned.1.call-update) | async-done | bytes 4194320 | tf_op jit(solution)/shard_map/all_gather | solution.py:13
  228.5 1.1 while.26
  228.5 1.0 bitcast_add_fusion.39
  230.3 70.9 %all-gather.13.cloned.1.call-done = f32[32,2,64,256]{3,2,1,0:T(8,128)} async-done(((f32[1,2,64,256]{3,2,1,0:T(8,128)}), f32[32,2,64,256]{3,2,1,0:T(8,128)}) %all-gather.13.cloned.1.call-update) | async-done | bytes 4194320 | tf_op jit(solution)/shard_map/all_gather | solution.py:13
  301.3 31.6 %while.27 = (s32[]{:T(128)}, f32[2]{0:T(128)S(1)}, f32[2,64,256]{2,1,0:T(8,128)S(1)}, s32[]{:T(128)}, f32[32,2]{1,0:T(8,128)S(1)}, /*index=5*/f32[32,2,64,256]{3...) while((s32[]{:T(128)}, f32[2]{0:T(128)S(1)}, f32[2,64,256]{2,1,0:T(8,128)S(1)}, s32[]{:T(128)}, ...), condition=%wide.region_3.4_spmd, body=%wide.region_2.3_spmd.sunk | while | flops 65544 | bytes 393411 | solution.py:22
  301.3 1.0 bitcast_add_fusion.40
  302.4 1.0 bitcast_add_fusion.40
  314.9 1.0 bitcast_add_fusion.40
  316.0 1.0 bitcast_add_fusion.40
  319.1 1.0 bitcast_add_fusion.40
  320.2 1.0 bitcast_add_fusion.40
  321.2 1.0 bitcast_add_fusion.40
  323.3 1.0 bitcast_add_fusion.40
  324.4 1.0 bitcast_add_fusion.40
  326.5 1.0 bitcast_add_fusion.40
  329.6 1.0 bitcast_add_fusion.40
  331.7 1.0 bitcast_add_fusion.40
  332.9 162.9 %all-reduce.2.cloned.1.call-done = f32[2,64,256]{2,1,0:T(8,128)} async-done(((f32[2,64,256]{2,1,0:T(8,128)}), f32[2,64,256]{2,1,0:T(8,128)}) %all-reduce.2.cloned.1.call-update) | async-done | bytes 131088 | tf_op jit(solution)/shard_map/psum | solution.py:27
  496.9 2.0 fusion.11
  499.7 5.9 %fusion.10 = f32[16,256,2,64]{1,3,2,0:T(8,128)S(1)} fusion(f32[16,2,256,64]{2,3,1,0:T(8,128)} %fusion, f32[16,2,64,256]{3,2,1,0:T(8,128)S(1)} %fusion.11, f32[16,256,256,1]{2,1,3,0:T(8,128)S(1)} %bitcast.168, f32[16,256,2]{1,2,0:T(2,128)S(1)} %copy.37), kind=kOutput, calls=%fused_computation.17 | convolution fusion | flops 1611661312 | bytes 10518528 | tf_op jit(solution)/shard_map/ghpn,gtn->gthp/dot_general | solution.py:103
  505.5 4.4 copy.64
  509.9 5.4 %reshape.801 = f32[4096,128]{1,0:T(8,128)} reshape(f32[16,256,2,64]{3,2,1,0:T(2,128)} %copy.64) | data formatting | bytes 4194304 | tf_op jit(solution)/shard_map/reshape | solution.py:106
  (118 shorter events, 37.3 us)
Async XLA Ops:
  6.5 76.0 %all-gather.9.cloned.1.call-start = ((), (), s32[]{:S(2)}) async-start(), calls=%async_computation.1 | async-start | bytes 4456448 | tf_op jit(solution)/shard_map/all_gather | solution.py:44
  7.3 154.8 %all-gather.7.cloned.1.call-start = ((), (), s32[]{:S(2)}) async-start(), calls=%async_computation | async-start | bytes 4456448 | tf_op jit(solution)/shard_map/all_gather | solution.py:45
  8.0 220.5 %all-gather.11.cloned.1.call-start = ((), (), s32[]{:S(2)}) async-start(), calls=%async_computation.2 | async-start | bytes 4325376 | tf_op jit(solution)/shard_map/all_gather | solution.py:13
  10.0 0.8 copy-start.3
  10.7 1.9 copy-start.1
  95.4 205.8 %all-gather.13.cloned.1.call-start = ((), (), s32[]{:S(2)}) async-start(), calls=%async_computation.3 | async-start | bytes 4325376 | tf_op jit(solution)/shard_map/all_gather | solution.py:13
  101.1 394.7 %all-reduce.2.cloned.1.call-start = ((), (), s32[]{:S(2)}) async-start(), calls=%async_computation.4 | async-start | bytes 262144 | tf_op jit(solution)/shard_map/psum | solution.py:27
  171.9 11.6 %copy-start.2 = (f32[16,8,16,256]{3,2,1,0:T(8,128)S(1)}, f32[16,8,16,256]{3,2,1,0:T(8,128)}, u32[]{:S(2)}) copy-start(f32[16,8,16,256]{3,2,1,0:T(8,128)} %copy-done.1) | copy-start | bytes 6291460
  496.9 2.8 copy-start
Sparse Core Ops, SparseCore 0:
  10.4 72.1 all-gather.8
  85.6 66.6 all-gather.6
  154.4 74.0 all-gather.10
  230.4 70.7 all-gather.12
  303.4 192.3 all-reduce.1
where the time goes:
time: 523 us; the launch traced here: 522 us
  waiting for transfers between devices  337 us (64%)
  blocking collectives  59.4 us (11%)
  other arithmetic  43.1 us (8%)
  matrix products  35.9 us (7%)
  local copies, waits for them, and re-layouts  31.7 us (6%)
  between operations  13.4 us (3%)
    psum x1, waiting for transfers between devices, from_root(): return lax.psum(kept, axis)  163 us
    all_gather x2, waiting for transfers between devices, prefix(): gathered = jax.tree.map(lambda a: lax.all_gather(a, axis), part)  104 us
    all_gather x1, waiting for transfers between devices, on_device(): lax.all_gather(b_proj, 'head', axis=1, tiled=True)  68.4 us
    all_gather x2, blocking collectives, prefix(): gathered = jax.tree.map(lambda a: lax.all_gather(a, axis), part)  59.4 us
    add x33, other arithmetic, combine(): jnp.exp(later[0])[:, None, None] * earlier[1] + later[1]  32.5 us
    dot_general x1, matrix products, on_device(): jnp.einsum('gtsh,gshp->gthp', weights, values, precision=highest_value)  11.8 us
    dot_general x1, matrix products, on_device(): jnp.einsum('gtn,gsn->gts', c_blocks, b_blocks, precision=highest_value)  11.6 us
  transfers between devices with their start and end apart: 5, of which 4 were waited for; matrix products, arithmetic and copies ran while one was open for 17% of the time, Pallas kernels for 0%

commit v1 on v0

v1 whole, which is shorter than its diff:
```python
import functools

import jax
import jax.numpy as jnp
from jax import lax
from jax.experimental import pallas as pl
from jax.experimental.pallas import tpu as pltpu
from jax.sharding import PartitionSpec as P

MESH = pl.DeviceIdType.MESH
F32 = jnp.float32
BF16 = jnp.bfloat16
L = 256
NBLK = 16
HALF_BLK = 8
N = 256
W = 128
TOK = 4096
NP = 4
PW = TOK // NP
PER = NBLK // NP
NSEQ = 32


def split2(a):
    hi = a.astype(BF16)
    return hi, (a - hi.astype(F32)).astype(BF16)


def split3(a):
    hi = a.astype(BF16)
    rest = a - hi.astype(F32)
    mid = rest.astype(BF16)
    return hi, mid, (rest - mid.astype(F32)).astype(BF16)


def dot(a, b):
    return jnp.dot(a, b, preferred_element_type=F32)


def dot3(ahi, alo, bhi, blo):
    return dot(ahi, bhi) + (dot(ahi, blo) + dot(alo, bhi))


def kernel(
    x_ref, b_ref, c_ref, ld_ref, o_ref,
    bt, ct, xv, xhi, xlo, xdhi, xdlo, chi, clo, dec, ecum, pre, out,
    cum, cumt, lanes, msg, recv, incs, inc,
    ssem, rsem, lsem, osem, asem,
):
    d = lax.axis_index("head")
    me = lax.axis_index("seq")
    y, x = d // 4, d % 4

    def at(fa, fo, so):
        if fa == 0:
            return ((y + so) % 4) * 4 + (x + fo) % 4
        return ((y + fo) % 4) * 4 + (x + so) % 4

    barrier = pltpu.get_barrier_semaphore()
    for fa in (0, 1):
        for o in (1, 3):
            pl.semaphore_signal(barrier, inc=1, device_id={"head": at(fa, o, 0)}, device_id_type=MESH)

    def greet(i, _):
        pl.semaphore_signal(barrier, inc=1, device_id={"seq": (me + i) % NSEQ}, device_id_type=MESH)
        return 0

    lax.fori_loop(1, NSEQ, greet, 0)
    own = [
        pltpu.make_async_copy(x_ref, xv, lsem.at[0]),
        pltpu.make_async_copy(b_ref, bt.at[pl.ds(pl.multiple_of(d * 16, 16), 16)], lsem.at[1]),
        pltpu.make_async_copy(c_ref, ct.at[pl.ds(pl.multiple_of(d * 16, 16), 16)], lsem.at[2]),
    ]
    for copy in own:
        copy.start()
    pl.semaphore_wait(barrier, NSEQ - 1 + 4)

    class Stage:
        def __init__(self, src, buf, which, c0, w, base):
            self.src, self.buf, self.which, self.c0, self.w, self.base = src, buf, which, c0, w, base

        def view(self, t, owner, part):
            start = self.c0 if part != 2 else self.c0 + self.w // 2
            width = self.w if part == 0 else self.w // 2
            return self.buf.at[pl.ds(pl.multiple_of(owner * 16 + 8 * t, 8), 8), pl.ds(start, width)]

        def copy(self, t, owner, target, part, k, from_src=False):
            dst = self.view(t, owner, part)
            src = self.src.at[pl.ds(8 * t, 8), pl.ds(self.c0, self.w)] if from_src else dst
            return pltpu.make_async_remote_copy(
                src, dst, ssem.at[self.which], rsem.at[self.base + t * 16 + k],
                device_id={"head": target}, device_id_type=MESH,
            )

        def send(self, *a, **k):
            self.copy(*a, **k).start()

        def wait(self, t, owner, part, k):
            self.copy(t, owner, d, part, k).wait_recv()

        def ev0(self):
            for t in (0, 1):
                self.send(t, d, at(t, 1, 0), 0, 0, from_src=True)
                self.send(t, d, at(t, 3, 0), 0, 1, from_src=True)
            for t in (0, 1):
                self.send(t, d, at(t, 0, 1), 0, 4, from_src=True)
                self.send(t, d, at(t, 0, 3), 0, 5, from_src=True)

        def ev1(self):
            for t in (0, 1):
                left, right = at(t, 3, 0), at(t, 1, 0)
                self.wait(t, left, 0, 0)
                self.send(t, left, right, 1, 2)
                self.wait(t, right, 0, 1)
                self.send(t, right, left, 2, 3)
                for q, owner in ((1, left), (2, right)):
                    self.send(t, owner, at(t, 0, 1), 0, 4 + 2 * q)
                    self.send(t, owner, at(t, 0, 3), 0, 5 + 2 * q)

        def ev2(self):
            for t in (0, 1):
                owner = at(t, 2, 0)
                self.wait(t, owner, 1, 2)
                self.wait(t, owner, 2, 3)
                self.send(t, owner, at(t, 0, 1), 0, 10)
                self.send(t, owner, at(t, 0, 3), 0, 11)

        def ev3(self, q):
            fo = (0, 3, 1, 2)[q]
            for t in (0, 1):
                down, up = at(t, fo, 3), at(t, fo, 1)
                self.wait(t, down, 0, 4 + 2 * q)
                self.wait(t, up, 0, 5 + 2 * q)
                if q < 2:
                    self.send(t, down, at(t, 0, 1), 0, 12 + q)
                else:
                    self.send(t, up, at(t, 0, 3), 0, 12 + q)

        def ev4(self):
            for q, fo in enumerate((0, 3, 1, 2)):
                for t in (0, 1):
                    self.wait(t, at(t, fo, 2), 0, 12 + q)

    def c_stage(p):
        return Stage(c_ref, ct, 1, pl.multiple_of(p * PW, PW), PW, 32 + p * 32)

    bst = Stage(b_ref, bt, 0, 0, TOK, 0)
    bst.ev0()

    lane = lax.broadcasted_iota(jnp.int32, (1, W), 1)
    first_head = lane < 64
    cum[...] = jnp.zeros_like(cum)
    for g in range(NBLK):
        for h in range(2):
            cum[h * 16 + g : h * 16 + g + 1, :] = ld_ref[h : h + 1, g * L : (g + 1) * L]
    r256 = lax.broadcasted_iota(jnp.int32, (L, L), 0)
    c256 = lax.broadcasted_iota(jnp.int32, (L, L), 1)
    upper = jnp.where(r256 <= c256, 1.0, 0.0).astype(BF16)
    total = sum(dot(part, upper) for part in split3(cum[...]))
    cum[...] = total
    turned = total.T
    for i, part in enumerate(split3(turned)):
        cumt[i] = part
    ends = jnp.broadcast_to(total[0:32, L - 1 : L], (32, W))
    ends = jnp.where(first_head, ends[0:16], ends[16:32])
    lanes[0:16] = jnp.exp(ends)
    sums = []
    for half in range(2):
        run = jnp.zeros((1, W), F32)
        for i in range(HALF_BLK):
            g = half * HALF_BLK + i
            lanes[16 + g : 17 + g, :] = jnp.exp(run)
            run = run + ends[g : g + 1]
        sums.append(jnp.exp(run))
    tail = jnp.concatenate(sums + [jnp.zeros((6, W), F32)], axis=0)
    own[0].wait()

    pick_row = lax.broadcasted_iota(jnp.int32, (W, W), 0)
    pick_lane = lax.broadcasted_iota(jnp.int32, (W, W), 1)

    def column(g, h):
        row = jnp.where(pick_lane < 64, g, 16 + g) if h is None else h * 16 + g
        sel = jnp.where(pick_row == row, 1.0, 0.0).astype(BF16)
        return dot(cumt[0], sel) + dot(cumt[1], sel) + dot(cumt[2], sel)

    def rows_of(g):
        return pl.ds(pl.multiple_of(g * L, L), L)

    def prepare(g, _):
        col = column(g, None)
        ecum[rows_of(g), :] = jnp.exp(col)
        val = xv[rows_of(g), :]
        xhi[rows_of(g), :], xlo[rows_of(g), :] = split2(val)
        to_end = jnp.exp(col[L - 1 : L, :] - col)
        xdhi[rows_of(g), :], xdlo[rows_of(g), :] = split2(val * to_end)
        return 0

    lax.fori_loop(0, NBLK, prepare, 0)

    def decay(g, _):
        for h in range(2):
            col = column(g, h)
            col = jnp.concatenate([col, col], axis=1)
            diff = col - cum[pl.ds(h * 16 + g, 1), :]
            dec[g, h] = jnp.exp(jnp.where(r256 >= c256, diff, -jnp.inf))
        return 0

    own[1].wait()
    bst.ev1()
    lax.fori_loop(0, 6, decay, 0)
    bst.ev2()

    def states(tiles):
        rows = [pl.ds(pl.multiple_of(k * 8, 8), 8) for k in tiles]
        for half in range(2):
            def step(i, run):
                g = half * HALF_BLK + i
                feats = jnp.concatenate([bt[r, rows_of(g)] for r in rows], axis=0)
                fhi, flo = split2(feats)
                for n, r in enumerate(rows):
                    pre[g, r, :] = run[n * 8 : n * 8 + 8]
                fresh = dot3(fhi, flo, xdhi[rows_of(g), :], xdlo[rows_of(g), :])
                return lanes[pl.ds(g, 1), :] * run + fresh

            run = lax.fori_loop(0, HALF_BLK, step, jnp.zeros((8 * len(tiles), W), F32))
            for n, k in enumerate(tiles):
                msg[k, half * 8 : half * 8 + 8, :] = run[n * 8 : n * 8 + 8]
        for k in tiles:
            msg[k, 16:24, :] = tail

            @pl.when(k != me)
            def _():
                pltpu.make_async_remote_copy(
                    msg.at[k], recv.at[me], asem.at[0], asem.at[1],
                    device_id={"seq": k}, device_id_type=MESH,
                ).start()

            @pl.when(k == me)
            def _():
                recv[k] = msg[k]

    def tiles(so):
        return [2 * at(t, fo, so) + t for t in (0, 1) for fo in range(4)]

    states(tiles(0))
    for q in range(4):
        bst.ev3(q)
        if q < 3:
            lax.fori_loop(6 + 3 * q, 9 + 3 * q, decay, 0)
    own[2].wait()
    c_stage(0).ev0()
    states(tiles(1) + tiles(3))
    lax.fori_loop(15, 16, decay, 0)
    bst.ev4()
    states(tiles(2))
    c_stage(0).ev1()
    c_stage(0).ev2()

    pltpu.make_async_copy(recv.at[pl.ds(0, NSEQ - 1)], recv.at[pl.ds(0, NSEQ - 1)], asem.at[1]).wait()

    def lower(j, run):
        incs[j, 0:8, :] = run
        return recv[j, 16:17, :] * run + recv[j, 0:8, :]

    def upper_step(i, run):
        j = NSEQ - 1 - i
        incs[j, 8:16, :] = run
        return recv[j, 17:18, :] * run + recv[j, 8:16, :]

    run = lax.fori_loop(0, NSEQ, lower, jnp.zeros((8, W), F32))
    lax.fori_loop(0, NSEQ, upper_step, run)
    inc[me] = incs[me]

    def give(i, _):
        j = (me + i) % NSEQ
        pltpu.make_async_remote_copy(
            incs.at[j], inc.at[me], asem.at[2], asem.at[3],
            device_id={"seq": j}, device_id_type=MESH,
        ).start()
        return 0

    lax.fori_loop(1, NSEQ, give, 0)
    for q in range(4):
        c_stage(0).ev3(q)
    c_stage(1).ev0()
    c_stage(0).ev4()

    def inside(g):
        turned = ct[:, rows_of(g)].T
        qhi, qlo = split2(turned)
        chi[rows_of(g), :], clo[rows_of(g), :] = qhi, qlo
        khi, klo = split2(bt[:, rows_of(g)])
        scores = dot3(qhi, qlo, khi, klo)
        vhi, vlo = xhi[rows_of(g), :], xlo[rows_of(g), :]
        acc = jnp.zeros((L, W), F32)
        for h in range(2):
            keep = first_head if h == 0 else jnp.logical_not(first_head)
            whi, wlo = split2(scores * dec[g, h])
            zero = jnp.zeros_like(vhi)
            acc = acc + dot3(whi, wlo, jnp.where(keep, vhi, zero), jnp.where(keep, vlo, zero))
        out[rows_of(g), :] = acc

    def carried(g, half):
        enter = lanes[pl.ds(16 + g, 1), :] * inc[:, half * 8 : half * 8 + 8, :].reshape(N, W) + pre[g]
        ehi, elo = split2(enter)
        z = dot3(chi[rows_of(g), :], clo[rows_of(g), :], ehi, elo)
        out[rows_of(g), :] = out[rows_of(g), :] + ecum[rows_of(g), :] * z

    def piece(p, _):
        g = p * PER
        nxt = c_stage(p + 1)
        inside(g)
        nxt.ev1()
        inside(g + 1)
        nxt.ev2()
        inside(g + 2)
        for q in range(4):
            nxt.ev3(q)

        @pl.when(p < NP - 2)
        def _():
            c_stage(p + 2).ev0()

        inside(g + 3)

        @pl.when(p < NP - 2)
        def _():
            nxt.ev4()

        return 0

    lax.fori_loop(0, NP - 1, piece, 0)
    pltpu.make_async_copy(inc.at[pl.ds(0, NSEQ - 1)], inc.at[pl.ds(0, NSEQ - 1)], asem.at[3]).wait()

    def carry_low(g, _):
        carried(g, 0)
        return 0

    def carry_high(g, _):
        carried(g, 1)
        return 0

    lax.fori_loop(0, HALF_BLK, carry_low, 0)
    lax.fori_loop(HALF_BLK, NBLK - PER, carry_high, 0)
    ahead = TOK - PW
    early = pltpu.make_async_copy(out.at[pl.ds(0, ahead)], o_ref.at[pl.ds(0, ahead)], osem.at[0])
    early.start()
    c_stage(NP - 1).ev4()

    def last(g, _):
        inside(g)
        carried(g, 1)
        return 0

    lax.fori_loop(NBLK - PER, NBLK, last, 0)
    late = pltpu.make_async_copy(out.at[pl.ds(ahead, PW)], o_ref.at[pl.ds(ahead, PW)], osem.at[1])
    late.start()

    for i, buf in enumerate((bt, ct)):
        sent = buf.at[pl.ds(0, 240)]
        pltpu.make_async_copy(sent, sent, ssem.at[i]).wait()
    for i, buf in ((0, msg), (2, incs)):
        sent = buf.at[pl.ds(0, NSEQ - 1)]
        pltpu.make_async_copy(sent, sent, asem.at[i]).wait()
    early.wait()
    late.wait()


def on_device(inputs, b_proj, c_proj, log_decay):
    vm = pltpu.VMEM
    return pl.pallas_call(
        kernel,
        out_shape=jax.ShapeDtypeStruct((TOK, W), F32),
        in_specs=[pl.BlockSpec(memory_space=pl.ANY)] * 3 + [pl.BlockSpec(memory_space=vm)],
        out_specs=pl.BlockSpec(memory_space=pl.ANY),
        scratch_shapes=[
            vm((N, TOK), F32), vm((N, TOK), F32),
            vm((TOK, W), F32),
            vm((TOK, W), BF16), vm((TOK, W), BF16),
            vm((TOK, W), BF16), vm((TOK, W), BF16),
            vm((TOK, N), BF16), vm((TOK, N), BF16),
            vm((NBLK, 2, L, L), F32),
            vm((TOK, W), F32),
            vm((NBLK, N, W), F32),
            vm((TOK, W), F32),
            vm((W, L), F32),
            vm((3, L, W), BF16),
            vm((32, W), F32),
            vm((NSEQ, 24, W), F32), vm((NSEQ, 24, W), F32),
            vm((NSEQ, 16, W), F32), vm((NSEQ, 16, W), F32),
            pltpu.SemaphoreType.DMA((2,)),
            pltpu.SemaphoreType.DMA((32 * (1 + NP),)),
            pltpu.SemaphoreType.DMA((3,)),
            pltpu.SemaphoreType.DMA((2,)),
            pltpu.SemaphoreType.DMA((4,)),
        ],
        compiler_params=pltpu.CompilerParams(
            collective_id=0, has_side_effects=True, vmem_limit_bytes=50 * 2**20
        ),
        cost_estimate=pl.CostEstimate(flops=5 * 10**9, bytes_accessed=2**23, transcendentals=3 * 10**6),
    )(inputs, b_proj.T, c_proj.T, log_decay.T)


def solution(mesh):
    return jax.shard_map(
        on_device,
        mesh=mesh,
        in_specs=(P("seq", "head"), P("seq", "head"), P("seq", "head"), P("seq", "head")),
        out_specs=P("seq", "head"),
        check_vma=False,
    )
```

time: 523 us -> 115 us (0.22)
  the two profiles are of different devices: /device:TPU:1 before, /device:TPU:320 now
where the time goes in v1:
time: 115 us
  Pallas kernels  111 us (97%)
  local copies, waits for them, and re-layouts  3.98 us (3%)
    pallas_call x1, Pallas kernels, on_device(): pl.pallas_call(kernel, out_shape=jax.ShapeDtypeStruct((TOK, W), F32), in_...  111 us
    unnamed x7, local copies, waits for them, and re-layouts  3.98 us

profile of v1, /device:TPU:320, one launch (start us, length us, event | category | flops | bytes accessed | tf_op | source)
XLA Modules:
  0.0 114.7 jit_solution(7833957822189181898)
XLA Ops:
  0.0 0.0 copy-start
  0.0 0.9 copy-done
  1.0 0.0 copy-start.1
  1.0 0.9 copy-done.1
  1.9 0.0 copy-start.2
  1.9 0.8 copy-done.2
  2.7 110.7 %shard_map.46 = f32[4096,128]{1,0:T(8,128)S(1)} custom-call(f32[4096,128]{1,0:T(8,128)} %x_ref.1, f32[16,4096]{1,0:T(8,128)S(1)} %bitcast.3, f32[16,4096]{1,0:T(8,128)S(1)} %bitcast.4, f32[2,4096]{1,0:T(2,128)S(1)} %bitcast.5), custom_call_target="tpu_custom_call" | custom-call | flops 5000000000 | bytes 8388608 | tf_op jit(solution)/shard_map/pallas_call | solution.py:372
  113.4 1.3 %copy.6 = f32[4096,128]{1,0:T(8,128)} copy(f32[4096,128]{1,0:T(8,128)S(1)} %shard_map.46) | data formatting | bytes 4194304
Async XLA Ops:
  0.0 0.9 copy-start
  1.0 0.9 copy-start.1
  1.9 0.8 copy-start.2

commit v2 on v1

--- a/solution.py
+++ b/solution.py
@@ -16,9 +16,7 @@
 N = 256
 W = 128
 TOK = 4096
-NP = 4
-PW = TOK // NP
-PER = NBLK // NP
+PIECES = (2048, 2048)
 NSEQ = 32
 
 
@@ -39,14 +37,15 @@
 
 
 def dot3(ahi, alo, bhi, blo):
-    return dot(ahi, bhi) + (dot(ahi, blo) + dot(alo, bhi))
+    left = jnp.concatenate([ahi, ahi, alo], axis=1)
+    return dot(left, jnp.concatenate([bhi, blo, bhi], axis=0))
 
 
 def kernel(
     x_ref, b_ref, c_ref, ld_ref, o_ref,
-    bt, ct, xv, xhi, xlo, xdhi, xdlo, chi, clo, dec, ecum, pre, out,
+    bt, ct, xv, xhi, xlo, xdhi, xdlo, chi, clo, khi, klo, dec, ecum, pre, out,
     cum, cumt, lanes, msg, recv, incs, inc,
-    ssem, rsem, lsem, osem, asem,
+    ssem, rsem, lsem, osem, asem, known,
 ):
     d = lax.axis_index("head")
     me = lax.axis_index("seq")
@@ -57,16 +56,27 @@
             return ((y + so) % 4) * 4 + (x + fo) % 4
         return ((y + fo) % 4) * 4 + (x + so) % 4
 
+    z, core = me // 2, me % 2
+    other = z * 2 + 1 - core
+
+    def along(o):
+        return ((z + o) % (NSEQ // 2)) * 2 + core
+
     barrier = pltpu.get_barrier_semaphore()
     for fa in (0, 1):
         for o in (1, 3):
             pl.semaphore_signal(barrier, inc=1, device_id={"head": at(fa, o, 0)}, device_id_type=MESH)
-
-    def greet(i, _):
-        pl.semaphore_signal(barrier, inc=1, device_id={"seq": (me + i) % NSEQ}, device_id_type=MESH)
-        return 0
-
-    lax.fori_loop(1, NSEQ, greet, 0)
+    for near in (along(1), along(-1 + NSEQ // 2), other):
+        pl.semaphore_signal(barrier, inc=1, device_id={"seq": near}, device_id_type=MESH)
+
+    def tell(r):
+        far = (along(1 << r), along(NSEQ // 2 - (1 << r))) if r < 3 else (other,)
+        for to in far:
+            pl.semaphore_signal(known.at[r], inc=1, device_id={"seq": to}, device_id_type=MESH)
+
+    def hear(r):
+        pl.semaphore_wait(known.at[r], 2 if r < 3 else 1)
+
     own = [
         pltpu.make_async_copy(x_ref, xv, lsem.at[0]),
         pltpu.make_async_copy(b_ref, bt.at[pl.ds(pl.multiple_of(d * 16, 16), 16)], lsem.at[1]),
@@ -74,7 +84,8 @@
     ]
     for copy in own:
         copy.start()
-    pl.semaphore_wait(barrier, NSEQ - 1 + 4)
+    pl.semaphore_wait(barrier, 7)
+    tell(0)
 
     class Stage:
         def __init__(self, src, buf, which, c0, w, base):
@@ -132,7 +143,7 @@
                 down, up = at(t, fo, 3), at(t, fo, 1)
                 self.wait(t, down, 0, 4 + 2 * q)
                 self.wait(t, up, 0, 5 + 2 * q)
-                if q < 2:
+                if q in (0, 3):
                     self.send(t, down, at(t, 0, 1), 0, 12 + q)
                 else:
                     self.send(t, up, at(t, 0, 3), 0, 12 + q)
@@ -142,9 +153,8 @@
                 for t in (0, 1):
                     self.wait(t, at(t, fo, 2), 0, 12 + q)
 
-    def c_stage(p):
-        return Stage(c_ref, ct, 1, pl.multiple_of(p * PW, PW), PW, 32 + p * 32)
-
+    starts = [sum(PIECES[:i]) for i in range(len(PIECES))]
+    cst = [Stage(c_ref, ct, 1, starts[i], w, 32 + i * 32) for i, w in enumerate(PIECES)]
     bst = Stage(b_ref, bt, 0, 0, TOK, 0)
     bst.ev0()
 
@@ -206,11 +216,6 @@
             dec[g, h] = jnp.exp(jnp.where(r256 >= c256, diff, -jnp.inf))
         return 0
 
-    own[1].wait()
-    bst.ev1()
-    lax.fori_loop(0, 6, decay, 0)
-    bst.ev2()
-
     def states(tiles):
         rows = [pl.ds(pl.multiple_of(k * 8, 8), 8) for k in tiles]
         for half in range(2):
@@ -226,6 +231,8 @@
             run = lax.fori_loop(0, HALF_BLK, step, jnp.zeros((8 * len(tiles), W), F32))
             for n, k in enumerate(tiles):
                 msg[k, half * 8 : half * 8 + 8, :] = run[n * 8 : n * 8 + 8]
+
+    def ship(tiles):
         for k in tiles:
             msg[k, 16:24, :] = tail
 
@@ -243,20 +250,50 @@
     def tiles(so):
         return [2 * at(t, fo, so) + t for t in (0, 1) for fo in range(4)]
 
+    def keys(g, _):
+        khi[:, rows_of(g)], klo[:, rows_of(g)] = split2(bt[:, rows_of(g)])
+        return 0
+
+    last = len(PIECES) - 1
+
+    def rest(p):
+        for q in (1, 2, 3):
+            cst[p].ev3(q)
+
+    own[1].wait()
+    hear(0)
+    tell(1)
+    bst.ev1()
+    lax.fori_loop(0, 3, decay, 0)
+    bst.ev3(0)
+    bst.ev2()
+    own[2].wait()
+    cst[0].ev0()
+    hear(1)
+    tell(2)
     states(tiles(0))
-    for q in range(4):
+    lax.fori_loop(3, 6, decay, 0)
+    for q in (1, 2, 3):
         bst.ev3(q)
-        if q < 3:
-            lax.fori_loop(6 + 3 * q, 9 + 3 * q, decay, 0)
-    own[2].wait()
-    c_stage(0).ev0()
+    cst[0].ev1()
+    cst[1].ev0()
+    hear(2)
+    tell(3)
     states(tiles(1) + tiles(3))
-    lax.fori_loop(15, 16, decay, 0)
+    hear(3)
+    ship(tiles(0) + tiles(1) + tiles(3))
     bst.ev4()
     states(tiles(2))
-    c_stage(0).ev1()
-    c_stage(0).ev2()
-
+    ship(tiles(2))
+    cst[0].ev3(0)
+    cst[0].ev2()
+    cst[1].ev1()
+    lax.fori_loop(6, 11, decay, 0)
+    rest(0)
+    if last > 1:
+        cst[2].ev0()
+    lax.fori_loop(11, NBLK, decay, 0)
+    lax.fori_loop(0, 4, keys, 0)
     pltpu.make_async_copy(recv.at[pl.ds(0, NSEQ - 1)], recv.at[pl.ds(0, NSEQ - 1)], asem.at[1]).wait()
 
     def lower(j, run):
@@ -281,80 +318,64 @@
         return 0
 
     lax.fori_loop(1, NSEQ, give, 0)
-    for q in range(4):
-        c_stage(0).ev3(q)
-    c_stage(1).ev0()
-    c_stage(0).ev4()
+    cst[1].ev3(0)
+    cst[1].ev2()
+    lax.fori_loop(4, NBLK, keys, 0)
+    cst[0].ev4()
 
     def inside(g):
         turned = ct[:, rows_of(g)].T
         qhi, qlo = split2(turned)
         chi[rows_of(g), :], clo[rows_of(g), :] = qhi, qlo
-        khi, klo = split2(bt[:, rows_of(g)])
-        scores = dot3(qhi, qlo, khi, klo)
+        scores = dot3(qhi, qlo, khi[:, rows_of(g)], klo[:, rows_of(g)])
         vhi, vlo = xhi[rows_of(g), :], xlo[rows_of(g), :]
-        acc = jnp.zeros((L, W), F32)
-        for h in range(2):
-            keep = first_head if h == 0 else jnp.logical_not(first_head)
-            whi, wlo = split2(scores * dec[g, h])
-            zero = jnp.zeros_like(vhi)
-            acc = acc + dot3(whi, wlo, jnp.where(keep, vhi, zero), jnp.where(keep, vlo, zero))
-        out[rows_of(g), :] = acc
-
-    def carried(g, half):
-        enter = lanes[pl.ds(16 + g, 1), :] * inc[:, half * 8 : half * 8 + 8, :].reshape(N, W) + pre[g]
+        heads = [dot3(*split2(scores * dec[g, h]), vhi, vlo) for h in range(2)]
+        out[rows_of(g), :] = jnp.where(first_head, heads[0], heads[1])
+
+    def carried(g):
+        half = g // HALF_BLK
+        enter = lanes[pl.ds(16 + g, 1), :] * inc[:, pl.ds(pl.multiple_of(half * 8, 8), 8), :].reshape(N, W) + pre[g]
         ehi, elo = split2(enter)
         z = dot3(chi[rows_of(g), :], clo[rows_of(g), :], ehi, elo)
         out[rows_of(g), :] = out[rows_of(g), :] + ecum[rows_of(g), :] * z
 
-    def piece(p, _):
-        g = p * PER
-        nxt = c_stage(p + 1)
+    def only_inside(g, _):
         inside(g)
-        nxt.ev1()
-        inside(g + 1)
-        nxt.ev2()
-        inside(g + 2)
-        for q in range(4):
-            nxt.ev3(q)
-
-        @pl.when(p < NP - 2)
-        def _():
-            c_stage(p + 2).ev0()
-
-        inside(g + 3)
-
-        @pl.when(p < NP - 2)
-        def _():
-            nxt.ev4()
-
-        return 0
-
-    lax.fori_loop(0, NP - 1, piece, 0)
+        return 0
+
+    def only_carried(g, _):
+        carried(g)
+        return 0
+
+    def both(g, _):
+        inside(g)
+        carried(g)
+        return 0
+
+    for p in range(last):
+        groups = [lambda p=p: rest(p + 1)]
+        if p + 3 <= last:
+            groups[0] = lambda p=p: (rest(p + 1), cst[p + 3].ev0())
+        if p + 2 <= last:
+            groups += [cst[p + 2].ev1, lambda p=p: (cst[p + 2].ev3(0), cst[p + 2].ev2())]
+        g = starts[p] // L
+        for group in groups:
+            inside(g)
+            g += 1
+            group()
+        lax.fori_loop(g, starts[p + 1] // L, only_inside, 0)
+        if p + 1 < last:
+            cst[p + 1].ev4()
+    ahead = starts[last]
     pltpu.make_async_copy(inc.at[pl.ds(0, NSEQ - 1)], inc.at[pl.ds(0, NSEQ - 1)], asem.at[3]).wait()
-
-    def carry_low(g, _):
-        carried(g, 0)
-        return 0
-
-    def carry_high(g, _):
-        carried(g, 1)
-        return 0
-
-    lax.fori_loop(0, HALF_BLK, carry_low, 0)
-    lax.fori_loop(HALF_BLK, NBLK - PER, carry_high, 0)
-    ahead = TOK - PW
+    lax.fori_loop(0, ahead // L, only_carried, 0)
     early = pltpu.make_async_copy(out.at[pl.ds(0, ahead)], o_ref.at[pl.ds(0, ahead)], osem.at[0])
     early.start()
-    c_stage(NP - 1).ev4()
-
-    def last(g, _):
-        inside(g)
-        carried(g, 1)
-        return 0
-
-    lax.fori_loop(NBLK - PER, NBLK, last, 0)
-    late = pltpu.make_async_copy(out.at[pl.ds(ahead, PW)], o_ref.at[pl.ds(ahead, PW)], osem.at[1])
+    cst[last].ev4()
+    lax.fori_loop(ahead // L, NBLK, both, 0)
+    late = pltpu.make_async_copy(
+        out.at[pl.ds(ahead, TOK - ahead)], o_ref.at[pl.ds(ahead, TOK - ahead)], osem.at[1]
+    )
     late.start()
 
     for i, buf in enumerate((bt, ct)):
@@ -380,6 +401,7 @@
             vm((TOK, W), BF16), vm((TOK, W), BF16),
             vm((TOK, W), BF16), vm((TOK, W), BF16),
             vm((TOK, N), BF16), vm((TOK, N), BF16),
+            vm((N, TOK), BF16), vm((N, TOK), BF16),
             vm((NBLK, 2, L, L), F32),
             vm((TOK, W), F32),
             vm((NBLK, N, W), F32),
@@ -390,13 +412,14 @@
             vm((NSEQ, 24, W), F32), vm((NSEQ, 24, W), F32),
             vm((NSEQ, 16, W), F32), vm((NSEQ, 16, W), F32),
             pltpu.SemaphoreType.DMA((2,)),
-            pltpu.SemaphoreType.DMA((32 * (1 + NP),)),
+            pltpu.SemaphoreType.DMA((32 * (1 + len(PIECES)),)),
             pltpu.SemaphoreType.DMA((3,)),
             pltpu.SemaphoreType.DMA((2,)),
             pltpu.SemaphoreType.DMA((4,)),
+            pltpu.SemaphoreType.REGULAR((4,)),
         ],
         compiler_params=pltpu.CompilerParams(
-            collective_id=0, has_side_effects=True, vmem_limit_bytes=50 * 2**20
+            collective_id=0, has_side_effects=True, vmem_limit_bytes=54 * 2**20
         ),
         cost_estimate=pl.CostEstimate(flops=5 * 10**9, bytes_accessed=2**23, transcendentals=3 * 10**6),
     )(inputs, b_proj.T, c_proj.T, log_decay.T)

time: 115 us -> 86.7 us (0.75)
  the two profiles are of different devices: /device:TPU:320 before, /device:TPU:1 now
where the time goes in v2:
time: 86.7 us; the launch traced here: 86.1 us
  Pallas kernels  83 us (96%)
  local copies, waits for them, and re-layouts  3.05 us (4%)
    pallas_call x1, Pallas kernels, on_device(): pl.pallas_call(kernel, out_shape=jax.ShapeDtypeStruct((TOK, W), F32), in_...  83 us
    unnamed x1, local copies, waits for them, and re-layouts  3.05 us

profile of v2, /device:TPU:1, one launch (start us, length us, event | category | flops | bytes accessed | tf_op | source)
XLA Modules:
  0.0 86.1 jit_solution(16341445456116936376)
XLA Ops:
  0.0 83.0 %shard_map.46 = f32[4096,128]{1,0:T(8,128)} custom-call(f32[4096,128]{1,0:T(8,128)} %x_ref.1, f32[16,4096]{1,0:T(8,128)} %bitcast.3, f32[16,4096]{1,0:T(8,128)} %bitcast.4, f32[2,4096]{1,0:T(2,128)} %bitcast.5), custom_call_target="tpu_custom_call" | custom-call | flops 5000000000 | bytes 8388608 | tf_op jit(solution)/shard_map/pallas_call | solution.py:393
  83.0 3.0 %copy.6 = f32[4096,128]{1,0:T(8,128)} copy(f32[4096,128]{1,0:T(8,128)} %shard_map.46) | data formatting | bytes 4194304

commit v3 on v2

--- a/solution.py
+++ b/solution.py
@@ -16,8 +16,9 @@
 N = 256
 W = 128
 TOK = 4096
-PIECES = (2048, 2048)
+PIECES = (2560, 1536)
 NSEQ = 32
+NZ = 16
 
 
 def split2(a):
@@ -43,9 +44,9 @@
 
 def kernel(
     x_ref, b_ref, c_ref, ld_ref, o_ref,
-    bt, ct, xv, xhi, xlo, xdhi, xdlo, chi, clo, khi, klo, dec, ecum, pre, out,
-    cum, cumt, lanes, msg, recv, incs, inc,
-    ssem, rsem, lsem, osem, asem, known,
+    bt, ct, xv, xs, xd, chi, clo, khi, klo, dec, ecum, pre, out,
+    cum, cumt, lanes, msg, sib, comb, recv, incs, ret, give, got, inc, mine, theirs, pair, dk,
+    ssem, rsem, lsem, osem, asem, xsem, known,
 ):
     d = lax.axis_index("head")
     me = lax.axis_index("seq")
@@ -60,22 +61,26 @@
     other = z * 2 + 1 - core
 
     def along(o):
-        return ((z + o) % (NSEQ // 2)) * 2 + core
+        return ((z + o) % (NZ)) * 2 + core
 
     barrier = pltpu.get_barrier_semaphore()
     for fa in (0, 1):
         for o in (1, 3):
             pl.semaphore_signal(barrier, inc=1, device_id={"head": at(fa, o, 0)}, device_id_type=MESH)
-    for near in (along(1), along(-1 + NSEQ // 2), other):
+    for near in (along(1), along(-1 + NZ), other):
         pl.semaphore_signal(barrier, inc=1, device_id={"seq": near}, device_id_type=MESH)
 
     def tell(r):
-        far = (along(1 << r), along(NSEQ // 2 - (1 << r))) if r < 3 else (other,)
-        for to in far:
+        for to in (along(1 << r), along(NZ - (1 << r))):
             pl.semaphore_signal(known.at[r], inc=1, device_id={"seq": to}, device_id_type=MESH)
 
     def hear(r):
-        pl.semaphore_wait(known.at[r], 2 if r < 3 else 1)
+        pl.semaphore_wait(known.at[r], 2)
+
+    def to_other(src, dst, k):
+        return pltpu.make_async_remote_copy(
+            src, dst, xsem.at[0, k], xsem.at[1, k], device_id={"seq": other}, device_id_type=MESH
+        )
 
     own = [
         pltpu.make_async_copy(x_ref, xv, lsem.at[0]),
@@ -183,7 +188,8 @@
             lanes[16 + g : 17 + g, :] = jnp.exp(run)
             run = run + ends[g : g + 1]
         sums.append(jnp.exp(run))
-    tail = jnp.concatenate(sums + [jnp.zeros((6, W), F32)], axis=0)
+    mine[...] = jnp.concatenate(sums + [jnp.zeros((6, W), F32)], axis=0)
+    to_other(mine, theirs, 4).start()
     own[0].wait()
 
     pick_row = lax.broadcasted_iota(jnp.int32, (W, W), 0)
@@ -201,9 +207,12 @@
         col = column(g, None)
         ecum[rows_of(g), :] = jnp.exp(col)
         val = xv[rows_of(g), :]
-        xhi[rows_of(g), :], xlo[rows_of(g), :] = split2(val)
+        hi = val.astype(BF16).astype(F32)
+        lo = val - hi
+        xs[0, rows_of(g), :] = jnp.where(first_head, hi, pltpu.roll(lo, 64, 1)).astype(BF16)
+        xs[1, rows_of(g), :] = jnp.where(first_head, pltpu.roll(hi, 64, 1), lo).astype(BF16)
         to_end = jnp.exp(col[L - 1 : L, :] - col)
-        xdhi[rows_of(g), :], xdlo[rows_of(g), :] = split2(val * to_end)
+        xd[rows_of(g), :] = jnp.concatenate(split2(val * to_end), axis=1)
         return 0
 
     lax.fori_loop(0, NBLK, prepare, 0)
@@ -216,39 +225,73 @@
             dec[g, h] = jnp.exp(jnp.where(r256 >= c256, diff, -jnp.inf))
         return 0
 
-    def states(tiles):
-        rows = [pl.ds(pl.multiple_of(k * 8, 8), 8) for k in tiles]
+    second = (y, x)
+    first = (x, y)
+
+    def states(offsets):
+        tiles = [(t, fo, so) for so in offsets for t in (0, 1) for fo in range(4)]
+        rows = [pl.ds(pl.multiple_of(at(t, fo, so) * 16 + 8 * t, 8), 8) for t, fo, so in tiles]
         for half in range(2):
             def step(i, run):
                 g = half * HALF_BLK + i
                 feats = jnp.concatenate([bt[r, rows_of(g)] for r in rows], axis=0)
-                fhi, flo = split2(feats)
                 for n, r in enumerate(rows):
                     pre[g, r, :] = run[n * 8 : n * 8 + 8]
-                fresh = dot3(fhi, flo, xdhi[rows_of(g), :], xdlo[rows_of(g), :])
+                both = dot(jnp.concatenate(split2(feats), axis=0), xd[rows_of(g), :])
+                both = both[: feats.shape[0]] + both[feats.shape[0] :]
+                fresh = both[:, :W] + both[:, W:]
                 return lanes[pl.ds(g, 1), :] * run + fresh
 
             run = lax.fori_loop(0, HALF_BLK, step, jnp.zeros((8 * len(tiles), W), F32))
-            for n, k in enumerate(tiles):
-                msg[k, half * 8 : half * 8 + 8, :] = run[n * 8 : n * 8 + 8]
-
-    def ship(tiles):
-        for k in tiles:
-            msg[k, 16:24, :] = tail
-
-            @pl.when(k != me)
+            for n, (t, fo, so) in enumerate(tiles):
+                place = ((second[t] + so) % 4) * 4 + (first[t] + fo) % 4
+                msg[t, place, half * 8 : half * 8 + 8, :] = run[n * 8 : n * 8 + 8]
+
+    def group(so, kind):
+        sec = y + (x - y) * kind
+        return pl.ds(pl.multiple_of(((sec + so) % 4) * 4, 4), 4)
+
+    def swap(so):
+        g = group(so, 1 - core)
+        return to_other(msg.at[1 - core, g], sib.at[g], so)
+
+    def ship(so):
+        swap(so).wait_recv()
+        sec = y + (x - y) * core
+        lead = ((sec + so) % 4) * 4
+        for i in range(4):
+            p = lead + i
+            own_l, own_u = msg[core, p, 0:8, :], msg[core, p, 8:16, :]
+            sib_l, sib_u = sib[p, 0:8, :], sib[p, 8:16, :]
+            comb[p, 0:8, :] = jnp.where(
+                core == 1, mine[0:1, :] * sib_l + own_l, theirs[0:1, :] * own_l + sib_l
+            )
+            comb[p, 8:16, :] = jnp.where(
+                core == 0, mine[1:2, :] * sib_u + own_u, theirs[1:2, :] * own_u + sib_u
+            )
+
+            @pl.when(p != z)
             def _():
                 pltpu.make_async_remote_copy(
-                    msg.at[k], recv.at[me], asem.at[0], asem.at[1],
-                    device_id={"seq": k}, device_id_type=MESH,
+                    comb.at[p], recv.at[z], asem.at[0], asem.at[1],
+                    device_id={"seq": p * 2 + core}, device_id_type=MESH,
                 ).start()
 
-            @pl.when(k == me)
+            @pl.when(p == z)
             def _():
-                recv[k] = msg[k]
-
-    def tiles(so):
-        return [2 * at(t, fo, so) + t for t in (0, 1) for fo in range(4)]
+                recv[p] = comb[p]
+
+    def spread(src, dst, k):
+        for off in (8, 9, 7, 10, 6, 11, 5, 12, 4, 13, 3, 14, 2, 15, 1):
+            to = (z + off) % NZ
+            pltpu.make_async_remote_copy(
+                src(to), dst.at[z], asem.at[k], asem.at[k + 1],
+                device_id={"seq": to * 2 + core}, device_id_type=MESH,
+            ).start()
+
+    def arrived(buf, k):
+        part = buf.at[pl.ds(0, NZ - 1)]
+        pltpu.make_async_copy(part, part, asem.at[k]).wait()
 
     def keys(g, _):
         khi[:, rows_of(g)], klo[:, rows_of(g)] = split2(bt[:, rows_of(g)])
@@ -271,20 +314,28 @@
     cst[0].ev0()
     hear(1)
     tell(2)
-    states(tiles(0))
+    states((0,))
+    swap(0).start()
+    to_other(mine, theirs, 4).wait_recv()
+    pair[...] = mine[...] * theirs[...]
+    dk[z] = pair[...]
     lax.fori_loop(3, 6, decay, 0)
     for q in (1, 2, 3):
         bst.ev3(q)
     cst[0].ev1()
     cst[1].ev0()
     hear(2)
-    tell(3)
-    states(tiles(1) + tiles(3))
-    hear(3)
-    ship(tiles(0) + tiles(1) + tiles(3))
+    spread(lambda to: pair, dk, 4)
+    states((1, 3))
+    swap(1).start()
+    swap(3).start()
+    ship(0)
     bst.ev4()
-    states(tiles(2))
-    ship(tiles(2))
+    states((2,))
+    swap(2).start()
+    ship(1)
+    ship(3)
+    ship(2)
     cst[0].ev3(0)
     cst[0].ev2()
     cst[1].ev1()
@@ -294,30 +345,40 @@
         cst[2].ev0()
     lax.fori_loop(11, NBLK, decay, 0)
     lax.fori_loop(0, 4, keys, 0)
-    pltpu.make_async_copy(recv.at[pl.ds(0, NSEQ - 1)], recv.at[pl.ds(0, NSEQ - 1)], asem.at[1]).wait()
-
-    def lower(j, run):
+    def put(p, kind, tile):
+        shard = p + ((p % 4) * 4 + p // 4 - p) * kind
+        r = pl.ds(pl.multiple_of(shard * 16 + kind * 8, 8), 8)
+        inc[0, r, :] = tile[0:8]
+        inc[1, r, :] = tile[8:16]
+
+    def enter_chip(p, _):
+        low, high = ret[p, 0:8, :], ret[p, 8:16, :]
+        own_l = mine[0:1, :] * low + msg[core, p, 0:8, :]
+        own_u = mine[1:2, :] * high + msg[core, p, 8:16, :]
+        sib_l = theirs[0:1, :] * low + sib[p, 0:8, :]
+        sib_u = theirs[1:2, :] * high + sib[p, 8:16, :]
+        give[p, 0:8, :] = jnp.where(core == 0, own_l, low)
+        give[p, 8:16, :] = jnp.where(core == 0, high, own_u)
+        put(p, core, jnp.concatenate(
+            [jnp.where(core == 0, low, sib_l), jnp.where(core == 0, sib_u, high)], axis=0))
+        return 0
+
+    def enter_other(p, _):
+        put(p, 1 - core, got[p])
+        return 0
+
+    arrived(dk, 5)
+    arrived(recv, 1)
+    run = jnp.zeros((8, W), F32)
+    for j in range(NZ):
         incs[j, 0:8, :] = run
-        return recv[j, 16:17, :] * run + recv[j, 0:8, :]
-
-    def upper_step(i, run):
-        j = NSEQ - 1 - i
+        run = dk[j, 0:1, :] * run + recv[j, 0:8, :]
+    for j in reversed(range(NZ)):
         incs[j, 8:16, :] = run
-        return recv[j, 17:18, :] * run + recv[j, 8:16, :]
-
-    run = lax.fori_loop(0, NSEQ, lower, jnp.zeros((8, W), F32))
-    lax.fori_loop(0, NSEQ, upper_step, run)
-    inc[me] = incs[me]
-
-    def give(i, _):
-        j = (me + i) % NSEQ
-        pltpu.make_async_remote_copy(
-            incs.at[j], inc.at[me], asem.at[2], asem.at[3],
-            device_id={"seq": j}, device_id_type=MESH,
-        ).start()
-        return 0
-
-    lax.fori_loop(1, NSEQ, give, 0)
+        run = dk[j, 1:2, :] * run + recv[j, 8:16, :]
+    spread(lambda to: incs.at[to], ret, 2)
+    ret[z] = incs[z]
+
     cst[1].ev3(0)
     cst[1].ev2()
     lax.fori_loop(4, NBLK, keys, 0)
@@ -328,27 +389,28 @@
         qhi, qlo = split2(turned)
         chi[rows_of(g), :], clo[rows_of(g), :] = qhi, qlo
         scores = dot3(qhi, qlo, khi[:, rows_of(g)], klo[:, rows_of(g)])
-        vhi, vlo = xhi[rows_of(g), :], xlo[rows_of(g), :]
-        heads = [dot3(*split2(scores * dec[g, h]), vhi, vlo) for h in range(2)]
-        out[rows_of(g), :] = jnp.where(first_head, heads[0], heads[1])
+        sums = []
+        for h in range(2):
+            weights = jnp.concatenate(split2(scores * dec[g, h]), axis=1)
+            vals = xs[h, rows_of(g), :]
+            sums.append(dot(weights, jnp.concatenate([vals, vals], axis=0)))
+        out[rows_of(g), :] = jnp.where(first_head, sums[0], sums[1]) + pltpu.roll(
+            jnp.where(first_head, sums[1], sums[0]), 64, 1
+        )
 
     def carried(g):
         half = g // HALF_BLK
-        enter = lanes[pl.ds(16 + g, 1), :] * inc[:, pl.ds(pl.multiple_of(half * 8, 8), 8), :].reshape(N, W) + pre[g]
+        enter = lanes[pl.ds(16 + g, 1), :] * inc[half] + pre[g]
         ehi, elo = split2(enter)
-        z = dot3(chi[rows_of(g), :], clo[rows_of(g), :], ehi, elo)
-        out[rows_of(g), :] = out[rows_of(g), :] + ecum[rows_of(g), :] * z
+        part = dot(chi[rows_of(g), :], jnp.concatenate([ehi, elo], axis=1))
+        part = part[:, :W] + (part[:, W:] + dot(clo[rows_of(g), :], ehi))
+        out[rows_of(g), :] = out[rows_of(g), :] + ecum[rows_of(g), :] * part
 
     def only_inside(g, _):
         inside(g)
         return 0
 
     def only_carried(g, _):
-        carried(g)
-        return 0
-
-    def both(g, _):
-        inside(g)
         carried(g)
         return 0
 
@@ -359,33 +421,38 @@
         if p + 2 <= last:
             groups += [cst[p + 2].ev1, lambda p=p: (cst[p + 2].ev3(0), cst[p + 2].ev2())]
         g = starts[p] // L
-        for group in groups:
+        for events in groups:
             inside(g)
             g += 1
-            group()
-        lax.fori_loop(g, starts[p + 1] // L, only_inside, 0)
+            events()
+        lax.fori_loop(g, starts[p + 1] // L, only_inside, 0, unroll=2)
         if p + 1 < last:
             cst[p + 1].ev4()
-    ahead = starts[last]
-    pltpu.make_async_copy(inc.at[pl.ds(0, NSEQ - 1)], inc.at[pl.ds(0, NSEQ - 1)], asem.at[3]).wait()
-    lax.fori_loop(0, ahead // L, only_carried, 0)
-    early = pltpu.make_async_copy(out.at[pl.ds(0, ahead)], o_ref.at[pl.ds(0, ahead)], osem.at[0])
-    early.start()
     cst[last].ev4()
-    lax.fori_loop(ahead // L, NBLK, both, 0)
-    late = pltpu.make_async_copy(
-        out.at[pl.ds(ahead, TOK - ahead)], o_ref.at[pl.ds(ahead, TOK - ahead)], osem.at[1]
-    )
-    late.start()
+    lax.fori_loop(starts[last] // L, NBLK, only_inside, 0, unroll=2)
+    arrived(ret, 3)
+    lax.fori_loop(0, NZ, enter_chip, 0)
+    to_other(give, got, 5).start()
+    to_other(give, got, 5).wait_recv()
+    lax.fori_loop(0, NZ, enter_other, 0)
+    halves = []
+    for i in range(2):
+        lax.fori_loop(i * HALF_BLK, (i + 1) * HALF_BLK, only_carried, 0, unroll=4)
+        part = pl.ds(i * TOK // 2, TOK // 2)
+        halves.append(pltpu.make_async_copy(out.at[part], o_ref.at[part], osem.at[i]))
+        halves[-1].start()
 
     for i, buf in enumerate((bt, ct)):
         sent = buf.at[pl.ds(0, 240)]
         pltpu.make_async_copy(sent, sent, ssem.at[i]).wait()
-    for i, buf in ((0, msg), (2, incs)):
-        sent = buf.at[pl.ds(0, NSEQ - 1)]
-        pltpu.make_async_copy(sent, sent, asem.at[i]).wait()
-    early.wait()
-    late.wait()
+    for i, buf in ((0, comb), (2, incs), (4, dk)):
+        arrived(buf, i)
+    for so in range(4):
+        swap(so).wait_send()
+    to_other(mine, theirs, 4).wait_send()
+    to_other(give, got, 5).wait_send()
+    for copy in halves:
+        copy.wait()
 
 
 def on_device(inputs, b_proj, c_proj, log_decay):
@@ -398,8 +465,8 @@
         scratch_shapes=[
             vm((N, TOK), F32), vm((N, TOK), F32),
             vm((TOK, W), F32),
-            vm((TOK, W), BF16), vm((TOK, W), BF16),
-            vm((TOK, W), BF16), vm((TOK, W), BF16),
+            vm((2, TOK, W), BF16),
+            vm((TOK, 2 * W), BF16),
             vm((TOK, N), BF16), vm((TOK, N), BF16),
             vm((N, TOK), BF16), vm((N, TOK), BF16),
             vm((NBLK, 2, L, L), F32),
@@ -409,14 +476,20 @@
             vm((W, L), F32),
             vm((3, L, W), BF16),
             vm((32, W), F32),
-            vm((NSEQ, 24, W), F32), vm((NSEQ, 24, W), F32),
-            vm((NSEQ, 16, W), F32), vm((NSEQ, 16, W), F32),
+            vm((2, NZ, 16, W), F32), vm((NZ, 16, W), F32),
+            vm((NZ, 16, W), F32), vm((NZ, 16, W), F32),
+            vm((NZ, 16, W), F32), vm((NZ, 16, W), F32),
+            vm((NZ, 16, W), F32), vm((NZ, 16, W), F32),
+            vm((2, N, W), F32),
+            vm((8, W), F32), vm((8, W), F32), vm((8, W), F32),
+            vm((NZ, 8, W), F32),
             pltpu.SemaphoreType.DMA((2,)),
             pltpu.SemaphoreType.DMA((32 * (1 + len(PIECES)),)),
             pltpu.SemaphoreType.DMA((3,)),
             pltpu.SemaphoreType.DMA((2,)),
-            pltpu.SemaphoreType.DMA((4,)),
-            pltpu.SemaphoreType.REGULAR((4,)),
+            pltpu.SemaphoreType.DMA((6,)),
+            pltpu.SemaphoreType.DMA((2, 6)),
+            pltpu.SemaphoreType.REGULAR((3,)),
         ],
         compiler_params=pltpu.CompilerParams(
             collective_id=0, has_side_effects=True, vmem_limit_bytes=54 * 2**20

time: 86.7 us -> 77.4 us (0.89)
  Pallas kernels: 83 us -> 74.1 us
    pallas_call x1, Pallas kernels: 83 us -> 74.1 us  [on_device(): pl.pallas_call(kernel, out_shape=jax.ShapeDtypeStruct((TOK, W), F32), in_...]
where the time goes in v3:
time: 77.4 us; the launch traced here: 77.2 us
  Pallas kernels  74.1 us (96%)
  local copies, waits for them, and re-layouts  3.05 us (4%)
    pallas_call x1, Pallas kernels, on_device(): pl.pallas_call(kernel, out_shape=jax.ShapeDtypeStruct((TOK, W), F32), in_...  74.1 us
    unnamed x1, local copies, waits for them, and re-layouts  3.05 us

profile of v3, /device:TPU:1, one launch (start us, length us, event | category | flops | bytes accessed | tf_op | source)
XLA Modules:
  0.0 77.2 jit_solution(16989999826957626971)
XLA Ops:
  0.0 74.1 %shard_map.46 = f32[4096,128]{1,0:T(8,128)} custom-call(f32[4096,128]{1,0:T(8,128)} %x_ref.1, f32[16,4096]{1,0:T(8,128)} %bitcast.3, f32[16,4096]{1,0:T(8,128)} %bitcast.4, f32[2,4096]{1,0:T(2,128)} %bitcast.5), custom_call_target="tpu_custom_call" | custom-call | flops 5000000000 | bytes 8388608 | tf_op jit(solution)/shard_map/pallas_call | solution.py:460
  74.1 3.0 %copy.6 = f32[4096,128]{1,0:T(8,128)} copy(f32[4096,128]{1,0:T(8,128)} %shard_map.46) | data formatting | bytes 4194304

commit v4 on v3

--- a/solution.py
+++ b/solution.py
@@ -431,10 +431,10 @@
     cst[last].ev4()
     lax.fori_loop(starts[last] // L, NBLK, only_inside, 0, unroll=2)
     arrived(ret, 3)
-    lax.fori_loop(0, NZ, enter_chip, 0)
+    lax.fori_loop(0, NZ, enter_chip, 0, unroll=4)
     to_other(give, got, 5).start()
     to_other(give, got, 5).wait_recv()
-    lax.fori_loop(0, NZ, enter_other, 0)
+    lax.fori_loop(0, NZ, enter_other, 0, unroll=4)
     halves = []
     for i in range(2):
         lax.fori_loop(i * HALF_BLK, (i + 1) * HALF_BLK, only_carried, 0, unroll=4)

time: 77.4 us -> 77.2 us (level)
  no operation moved by 1% of the time
where the time goes in v4:
time: 77.2 us; the launch traced here: 77 us
  Pallas kernels  74 us (96%)
  local copies, waits for them, and re-layouts  3.05 us (4%)
    pallas_call x1, Pallas kernels, on_device(): pl.pallas_call(kernel, out_shape=jax.ShapeDtypeStruct((TOK, W), F32), in_...  74 us
    unnamed x1, local copies, waits for them, and re-layouts  3.05 us

profile of v4, /device:TPU:1, one launch (start us, length us, event | category | flops | bytes accessed | tf_op | source)
XLA Modules:
  0.0 77.0 jit_solution(18385934363123605717)
XLA Ops:
  0.0 74.0 %shard_map.46 = f32[4096,128]{1,0:T(8,128)} custom-call(f32[4096,128]{1,0:T(8,128)} %x_ref.1, f32[16,4096]{1,0:T(8,128)} %bitcast.3, f32[16,4096]{1,0:T(8,128)} %bitcast.4, f32[2,4096]{1,0:T(2,128)} %bitcast.5), custom_call_target="tpu_custom_call" | custom-call | flops 5000000000 | bytes 8388608 | tf_op jit(solution)/shard_map/pallas_call | solution.py:460
  74.0 3.0 %copy.6 = f32[4096,128]{1,0:T(8,128)} copy(f32[4096,128]{1,0:T(8,128)} %shard_map.46) | data formatting | bytes 4194304
